TPU v7x, 32 devices: a whole 2x2x4 slice. The times are simulated.
32 devices in a mesh: dp: 4 (over z), ctx: 8 (over y, x, core).
Axes of the slice: x: 2, y: 2, z: 4, core: 2. Of those that a mesh axis runs over, the one named last changes fastest.
Arguments:
- query_heads: bfloat16 [4, 1024, 1024], P('dp', 'ctx'), may hold values from -6 to 6
- key_heads: bfloat16 [4, 1024, 1024], P('dp', 'ctx'), may hold values from -6 to 6
- value_heads: bfloat16 [4, 1024, 1024], P('dp', 'ctx'), may hold values from -6 to 6
- grad_output: bfloat16 [4, 1024, 1024], P('dp', 'ctx'), may hold values from -6 to 6
- layer_input: bfloat16 [4, 1024, 1152], P('dp', 'ctx'), may hold values from -6 to 6
Outputs:
- grad_query: bfloat16 [4, 1024, 1024], P('dp', 'ctx')
- grad_key: bfloat16 [4, 1024, 1024], P('dp', 'ctx')
- grad_value: bfloat16 [4, 1024, 1024], P('dp', 'ctx')
- grad_weight: float32 [1152, 1024], P('dp', 'ctx')
All inputs are finite; a program needn't handle non-finite values.
Results may differ from a plain program's by a relative error of at most 0.008.
Values sent between devices are 32-bit elements; how exact they have to be, the bound alone decides.
A program may use at most 128 MiB of HBM per device.

v0:
```python
import math

import jax
import jax.numpy as jnp
from jax import lax
from jax.sharding import PartitionSpec as P

HD = 128
HV = 8
DW = 1152


def entering(part, axis, combine, identity, reverse):
    count = lax.axis_size(axis)
    place = lax.axis_index(axis)
    ahead = count - 1 - place if reverse else place
    gathered = lax.all_gather(part, axis)
    state = jnp.zeros_like(part) + jnp.asarray(identity, part.dtype)

    def one(step, state):
        source = count - 1 - step if reverse else step
        return combine(state, lax.dynamic_index_in_dim(gathered, source, 0, False))

    return lax.fori_loop(0, ahead, one, state)


def add_states(earlier, later):
    return earlier + later


def apply_state(rows_in, state, form):
    upper_part = state.astype(jnp.bfloat16)
    lower_part = (state - upper_part.astype(jnp.float32)).astype(jnp.bfloat16)
    first = jnp.einsum(form, rows_in, upper_part, preferred_element_type=jnp.float32)
    return first + jnp.einsum(form, rows_in, lower_part, preferred_element_type=jnp.float32)


def on_device(query_heads, key_heads, value_heads, grad_output, layer_input):
    length = query_heads.shape[1]
    ctx_count = lax.axis_size("ctx")
    dp_count = lax.axis_size("dp")
    scale = 1.0 / math.sqrt(HD * length * ctx_count)
    rscale = 1.0 / math.sqrt(dp_count * length * ctx_count)
    query = query_heads[0].reshape(length, HV, HD)
    keyed = key_heads[0].reshape(length, HV, HD)
    valued = value_heads[0].reshape(length, HV, HD)
    cotan = grad_output[0].reshape(length, HV, HD)
    kv_block = jnp.einsum("thi,thj->hij", keyed, valued, preferred_element_type=jnp.float32)
    qg_block = jnp.einsum("thi,thj->hij", query, cotan, preferred_element_type=jnp.float32)
    zeros = jnp.zeros((HV, HD, HD), jnp.float32)
    prefix = entering(kv_block, "ctx", add_states, zeros, False)
    suffix = entering(qg_block, "ctx", add_states, zeros, True)
    positions = jnp.arange(length)
    causal = (positions[:, None] >= positions[None, :]).astype(jnp.float32)
    score_raw = jnp.einsum("thd,shd->hts", query, keyed, preferred_element_type=jnp.float32)
    grad_raw = jnp.einsum("thd,shd->hts", cotan, valued, preferred_element_type=jnp.float32)
    score_w = (scale * score_raw * causal).astype(jnp.bfloat16)
    grad_w = (scale * grad_raw * causal).astype(jnp.bfloat16)
    dquery = jnp.einsum("hts,shd->thd", grad_w, keyed, preferred_element_type=jnp.float32)
    dquery = dquery + scale * apply_state(cotan, prefix, "thj,hij->thi")
    dkey = jnp.einsum("hts,thd->shd", grad_w, query, preferred_element_type=jnp.float32)
    dkey = dkey + scale * apply_state(valued, suffix, "shj,hij->shi")
    dvalue = jnp.einsum("hts,thd->shd", score_w, cotan, preferred_element_type=jnp.float32)
    dvalue = dvalue + scale * apply_state(keyed, suffix, "shi,hij->shj")
    width = HV * HD
    dquery = dquery.reshape(1, length, width).astype(jnp.bfloat16)
    dkey = dkey.reshape(1, length, width).astype(jnp.bfloat16)
    dvalue = dvalue.reshape(length, width).astype(jnp.bfloat16)
    inputs = layer_input[0]
    col_block = width // ctx_count
    value_tiles = dvalue.reshape(length, ctx_count, col_block)
    term = (
        jnp.einsum("tr,tcw->crw", inputs, value_tiles, preferred_element_type=jnp.float32) * rscale
    )
    column_part = lax.psum_scatter(term, "ctx", scatter_dimension=0, tiled=True)
    weight_part = lax.psum_scatter(column_part, "dp", scatter_dimension=1, tiled=True)
    weight_part = weight_part.reshape(DW // dp_count, col_block)
    return (dquery, dkey, dvalue.reshape(1, length, width), weight_part)


def solution(mesh):
    in_specs = (
        P("dp", "ctx", None),
        P("dp", "ctx", None),
        P("dp", "ctx", None),
        P("dp", "ctx", None),
        P("dp", "ctx", None),
    )
    out_specs = (P("dp", "ctx", None), P("dp", "ctx", None), P("dp", "ctx", None), P("dp", "ctx"))
    return jax.shard_map(
        on_device, mesh=mesh, in_specs=in_specs, out_specs=out_specs, check_vma=False
    )
```

profile of v0, /device:TPU:0, one launch (start us, length us, event | category | flops | bytes accessed | tf_op | source)
XLA Modules:
  0.0 177.4 jit_solution(1471655008704773217)
XLA Ops:
  7.2 1.2 copy.54
  8.4 1.0 copy.57
  9.4 1.1 fusion.17
  10.6 1.0 copy.55
  11.6 1.0 copy.56
  12.6 1.1 fusion.25
  13.8 36.3 %all-gather.7.cloned.1.call-done = f32[64,128,128]{2,1,0:T(8,128)} async-done(((f32[8,128,128]{2,1,0:T(8,128)}), f32[64,128,128]{2,1,0:T(8,128)}) %all-gather.7.cloned.1.call-update) | async-done | bytes 4194320 | tf_op jit(solution)/shard_map/all_gather | solution.py:17
  50.2 8.4 %while.23 = (s32[]{:T(128)}, f32[8,128,128]{2,1,0:T(8,128)S(1)}, s32[]{:T(128)}, f32[8,8,128,128]{3,2,1,0:T(8,128)}, s32[]{:T(128)}, /*index=5*/s32[]{:T(128)}, s32[]{:T(128)}, s32[]{:T(128)}) while((s32[]{:T(128)}, f32[8,128,128]{2,1,0:T(8,128)S(1)}, s32[]{:T(128)}, f32[8,8,128,128]{3,2,1,0:T(8,128)}, s32[]{:T(128)}, /*index=5*/s32[]{:T(128)}, ...), condition=%wide.region_3.4_spmd, body=%wide.region_2.3_spmd.sunk | while | flops 131078 | bytes 1573007 | solution.py:24
  50.2 1.2 bitcast_add_fusion.5
  51.4 1.2 bitcast_add_fusion.5
  52.6 1.2 bitcast_add_fusion.5
  53.8 1.2 bitcast_add_fusion.5
  55.0 1.2 bitcast_add_fusion.5
  56.1 1.2 bitcast_add_fusion.5
  57.3 1.2 bitcast_add_fusion.5
  58.5 0.3 fusion.33
  58.9 0.3 fusion.5
  59.2 0.5 fusion.12
  59.7 2.9 %fusion = f32[8,1152,128]{1,2,0:T(8,128)} fusion(bf16[128,8,128]{0,2,1:T(8,128)(2,1)S(1)} %fusion.12, bf16[1,128,1152]{2,1,0:T(8,128)(2,1)S(1)} %copy-done), kind=kOutput, calls=%fused_computation.3 | convolution fusion | flops 303169536 | bytes 5275648 | tf_op jit(solution)/shard_map/tr,tcw->crw/dot_general | solution.py:73
  62.7 0.3 fusion.10
  63.0 25.8 %all-gather.5.cloned.1.call-done = f32[64,128,128]{2,1,0:T(8,128)} async-done(((f32[8,128,128]{2,1,0:T(8,128)}), f32[64,128,128]{2,1,0:T(8,128)}) %all-gather.5.cloned.1.call-update) | async-done | bytes 4194320 | tf_op jit(solution)/shard_map/all_gather | solution.py:17
  89.0 57.1 %reduce-scatter.3.cloned.1.call-done = f32[1,1152,128]{1,2,0:T(8,128)} async-done(((f32[8,1152,128]{1,2,0:T(8,128)}), f32[1,1152,128]{1,2,0:T(8,128)}) %reduce-scatter.3.cloned.1.call-update) | async-done | bytes 589840 | tf_op jit(solution)/shard_map/reduce_scatter | solution.py:75
  146.1 2.0 %copy.47 = f32[1,1152,128]{2,0,1:T(1,128)} copy(f32[1,1152,128]{1,2,0:T(8,128)} %reduce-scatter.3.cloned.1.call-done) | data formatting | bytes 1179648 | tf_op jit(solution)/shard_map/reduce_scatter | solution.py:75
  148.2 0.2 fusion.9
  148.4 0.3 fusion.14
  148.7 0.9 copy.48
  149.6 0.3 fusion.23
  149.9 0.3 fusion.7
  150.2 0.3 fusion.13
  150.5 0.8 copy.49
  151.3 0.8 copy.50
  152.2 18.7 %reduce-scatter.5.cloned.1.call-done = f32[1,288,128]{2,0,1:T(1,128)} async-done(((f32[1,1152,128]{2,0,1:T(1,128)}), f32[1,288,128]{2,0,1:T(1,128)}) %reduce-scatter.5.cloned.1.call-update) | async-done | bytes 147472 | tf_op jit(solution)/shard_map/reduce_scatter | solution.py:76
  (15 shorter events, 0.5 us)
Async XLA Ops:
  7.2 52.5 %copy-start = (bf16[1,128,1152]{2,1,0:T(8,128)(2,1)S(1)}, bf16[1,128,1152]{2,1,0:T(8,128)(2,1)}, u32[]{:S(2)}) copy-start(bf16[1,128,1152]{2,1,0:T(8,128)(2,1)} %param.13) | copy-start | bytes 884740
  7.2 42.9 %all-gather.7.cloned.1.call-start = ((), (), s32[]{:S(2)}) async-start(), calls=%async_computation.5 | async-start | bytes 4718592 | tf_op jit(solution)/shard_map/all_gather | solution.py:17
  10.6 78.2 %all-gather.5.cloned.1.call-start = ((), (), s32[]{:S(2)}) async-start(), calls=%async_computation.4 | async-start | bytes 4718592 | tf_op jit(solution)/shard_map/all_gather | solution.py:17
  13.7 132.4 %reduce-scatter.3.cloned.1.call-start = ((), (), s32[]{:S(2)}) async-start(), calls=%async_computation.2 | async-start | bytes 5308416 | tf_op jit(solution)/shard_map/reduce_scatter | solution.py:75
  62.6 108.3 %reduce-scatter.5.cloned.1.call-start = ((), (), s32[]{:S(2)}) async-start(), calls=%async_computation.3 | async-start | bytes 737280 | tf_op jit(solution)/shard_map/reduce_scatter | solution.py:76
Sparse Core Ops, SparseCore 0:
  10.7 39.4 all-gather.6
  52.0 36.7 all-gather.4
  92.2 53.8 reduce-scatter.2
  148.9 21.9 reduce-scatter.4
where the time goes:
time: 178 us; the launch traced here: 177 us
  waiting for transfers between devices  138 us (78%)
  between operations  13.9 us (8%)
  local copies, waits for them, and re-layouts  8.78 us (5%)
  matrix products  8.23 us (5%)
  other arithmetic  8.21 us (5%)
    all_gather x2, waiting for transfers between devices, entering(): gathered = lax.all_gather(part, axis)  62.1 us
    reduce_scatter x1, waiting for transfers between devices, on_device(): column_part = lax.psum_scatter(term, 'ctx', scatter_dimension=0, tiled=True)  57.1 us
    reduce_scatter x1, waiting for transfers between devices, on_device(): lax.psum_scatter(column_part, 'dp', scatter_dimension=1, tiled=True)  18.7 us
    add x7, other arithmetic, add_states(): return earlier + later  8.2 us
    unnamed x8, local copies, waits for them, and re-layouts  5.54 us
  transfers between devices with their start and end apart: 4, of which 4 were waited for; matrix products, arithmetic and copies ran while one was open for 11% of the time, Pallas kernels for 0%

commit v1 on v0

v1 whole, which is shorter than its diff:
```python
import functools
import math

import jax
import jax.numpy as jnp
from jax import lax
from jax.experimental import pallas as pl
from jax.experimental.pallas import tpu as pltpu
from jax.sharding import PartitionSpec as P

HD = 128
NN = (((1,), (0,)), ((), ()))
NT = (((1,), (1,)), ((), ()))
TN = (((0,), (0,)), ((), ()))


def dot(a, b, dims):
    return lax.dot_general(a, b, dims, preferred_element_type=jnp.float32)


def kernel(
    n, m, scale, rscale,
    q, k, v, g, x,
    dq, dk, dv, w,
    xg, xb, st, sib, tot, srecv, ext, acc, dvs, dvg, wt, wrecv,
    x_send, x_recv, p_send, p_recv, s_send, s_recv, e_send, e_recv,
    d_send, d_recv, w_send, w_recv,
):
    length, width = q.shape
    heads = width // HD
    half = heads // 2
    chips = n // 2
    cb = dvs.shape[2]
    rows = wt.shape[1]
    part = length // 2
    bits = n.bit_length() - 1
    me = lax.axis_index("ctx")
    row = lax.axis_index("dp")
    core = lax.rem(me, 2)
    chip = me // 2
    sibling = me + 1 - 2 * core

    def flip(index, mask):
        out = index
        for b in range(bits):
            if mask >> b & 1:
                out = out + (1 << b) * (1 - 2 * lax.rem(me // (1 << b), 2))
        return out

    def remote(src, dst, send, recv, to):
        return pltpu.make_async_remote_copy(
            src_ref=src, dst_ref=dst, send_sem=send, recv_sem=recv,
            device_id=to, device_id_type=pl.DeviceIdType.MESH,
        )

    orders = ([*range(1, bits), 0], [*range(bits - 1, 0, -1), 0])

    def x_copy(s, mask, b):
        slot = flip(me, mask)
        ref = xg.at[slot, pl.ds(s * part, part)]
        got = mask | (1 << b)
        return remote(
            ref, ref, x_send.at[s, got], x_recv.at[s, got], {"ctx": flip(me, 1 << b)}
        )

    def reached(s, mask):
        return max([i + 1 for i, b in enumerate(orders[s]) if mask >> b & 1], default=0)

    def x_wait(s, mask):
        last = orders[s][reached(s, mask) - 1]
        x_copy(s, mask ^ (1 << last), last).wait_recv()

    def x_forward(s, mask):
        for b in orders[s][reached(s, mask):]:
            x_copy(s, mask, b).start()

    barrier = pltpu.get_barrier_semaphore()
    for j in range(1, n):
        pl.semaphore_signal(
            barrier, inc=1, device_id={"ctx": lax.rem(me + j, n)},
            device_id_type=pl.DeviceIdType.MESH,
        )
    for j in range(1, m):
        pl.semaphore_signal(
            barrier, inc=1, device_id={"dp": lax.rem(row + j, m)},
            device_id_type=pl.DeviceIdType.MESH,
        )

    def cols(h):
        return slice(h * HD, (h + 1) * HD)

    for h in range(heads):
        a, i = h // half, h % half
        st[a, 0, i] = dot(k[:, cols(h)], v[:, cols(h)], TN)
        st[a, 1, i] = dot(q[:, cols(h)], g[:, cols(h)], TN)
    xg[me] = x[...].astype(jnp.float32)
    pl.semaphore_wait(barrier, n - 1 + m - 1)

    pair = [
        remote(st.at[1 - core], sib.at[1 - core], p_send.at[0], p_recv.at[0], {"ctx": sibling}),
        remote(st.at[core], sib.at[core], p_send.at[1], p_recv.at[1], {"ctx": sibling}),
    ]
    pair_in = remote(st.at[core], sib.at[core], p_send.at[0], p_recv.at[0], {"ctx": sibling})
    for c in pair:
        c.start()
    for s in range(2):
        x_copy(s, 0, orders[s][0]).start()
    pair_in.wait_recv()
    tot[...] = st[core] + sib[core]
    states = []
    for j in range(1, chips):
        wrap = (chip + j) // chips
        to = (chip + j - chips * wrap) * 2 + core
        c = remote(tot.at[wrap], srecv.at[j - 1], s_send.at[j - 1], s_recv.at[j - 1], {"ctx": to})
        c.start()
        states.append(c)
    for s in range(2):
        for b in orders[s][1:]:
            x_copy(s, 0, b).start()

    at_row = lax.broadcasted_iota(jnp.int32, (length, length), 0)
    at_col = lax.broadcasted_iota(jnp.int32, (length, length), 1)
    lower = at_row >= at_col
    upper = at_row <= at_col
    for h in range(heads):
        qh, kh, vh, gh = (r[:, cols(h)] for r in (q, k, v, g))
        score_t = jnp.where(upper, scale * dot(kh, qh, NT), 0.0).astype(jnp.bfloat16)
        grad = jnp.where(lower, scale * dot(gh, vh, NT), 0.0).astype(jnp.bfloat16)
        acc[0, :, cols(h)] = dot(grad, kh, NN)
        acc[1, :, cols(h)] = dot(grad, qh, TN)
        acc[2, :, cols(h)] = dot(score_t, gh, NN)

    if bits > 1:
        for s in range(2):
            mask = 1 << orders[s][0]
            x_wait(s, mask)
            x_forward(s, mask)

    ext[core] = jnp.zeros_like(tot)
    for j in range(1, chips):
        kind = 1 - (chip - j + chips) // chips
        states[j - 1].wait_recv()
        ext[core, kind] += srecv[j - 1]
    share = remote(ext.at[core], ext.at[core], e_send, e_recv, {"ctx": sibling})
    share_in = remote(ext.at[1 - core], ext.at[1 - core], e_send, e_recv, {"ctx": sibling})
    share.start()
    pair_rest = remote(st.at[1 - core], sib.at[1 - core], p_send.at[1], p_recv.at[1], {"ctx": sibling})
    pair_rest.wait_recv()
    share_in.wait_recv()

    second = core.astype(jnp.float32)
    first = 1.0 - second

    def suffix(h):
        a, i = h // half, h % half
        return (scale * (ext[a, 1, i] + first * sib[a, 1, i])).astype(jnp.bfloat16)

    def prefix(h):
        a, i = h // half, h % half
        return (scale * (ext[a, 0, i] + second * sib[a, 0, i])).astype(jnp.bfloat16)

    for h in range(heads):
        out = acc[2, :, cols(h)] + dot(k[:, cols(h)], suffix(h), NN)
        dv[:, cols(h)] = out.astype(jnp.bfloat16)
    for j in range(n):
        dvs[j] = dv[:, j * cb:(j + 1) * cb].astype(jnp.float32)
    values = []
    for j in range(1, n):
        to = lax.rem(me + j, n)
        c = remote(dvs.at[to], dvg.at[me], d_send.at[j - 1], d_recv.at[j - 1], {"ctx": to})
        c.start()
        values.append(c)
    dvg[me] = dvs[me]

    waited = [{1 << orders[s][0]} if bits > 1 else set() for s in range(2)]
    for i in range(1, bits - 1):
        for s in range(2):
            for mask in range(n):
                if reached(s, mask) == i + 1:
                    x_wait(s, mask)
                    x_forward(s, mask)
                    waited[s].add(mask)

    for h in range(heads):
        out = acc[0, :, cols(h)] + dot(g[:, cols(h)], prefix(h), NT)
        dq[:, cols(h)] = out.astype(jnp.bfloat16)
        out = acc[1, :, cols(h)] + dot(v[:, cols(h)], suffix(h), NT)
        dk[:, cols(h)] = out.astype(jnp.bfloat16)

    for mask in range(n):
        for s in range(2):
            if mask and mask not in waited[s]:
                x_wait(s, mask)
        slot = flip(me, mask)
        xb[slot] = xg[slot].astype(jnp.bfloat16)
    for j in range(1, n):
        came = lax.rem(me - j + n, n)
        remote(dvs.at[came], dvg.at[came], d_send.at[j - 1], d_recv.at[j - 1], {"ctx": came}).wait_recv()

    across = dvg[...].reshape(n * length, cb).astype(jnp.bfloat16)
    down = xb[...].reshape(n * length, xb.shape[2])
    total = jnp.transpose(dot(across, down, TN))
    for d in range(m):
        wt[d] = total[d * rows:(d + 1) * rows]
    weights = []
    for j in range(1, m):
        to = lax.rem(row + j, m)
        c = remote(wt.at[to], wrecv.at[j - 1], w_send.at[j - 1], w_recv.at[j - 1], {"dp": to})
        c.start()
        weights.append(c)
    out = wt[row]
    for c in weights:
        c.wait_recv()
    for j in range(1, m):
        out = out + wrecv[j - 1]
    w[...] = out * rscale

    for c in pair + states + [share] + values + weights:
        c.wait_send()
    for s in range(2):
        for mask in range(n):
            for b in orders[s][reached(s, mask):]:
                x_copy(s, mask, b).wait_send()


def on_device(query_heads, key_heads, value_heads, grad_output, layer_input):
    length, width = query_heads.shape[1:]
    wide = layer_input.shape[2]
    n = lax.axis_size("ctx")
    m = lax.axis_size("dp")
    scale = 1.0 / math.sqrt(HD * length * n)
    rscale = 1.0 / math.sqrt(m * length * n)
    heads, chips, cb, rows = width // HD, n // 2, width // n, wide // m
    half = heads // 2
    f32, bf16 = jnp.float32, jnp.bfloat16
    vmem = pl.BlockSpec(memory_space=pltpu.VMEM)
    dma = pltpu.SemaphoreType.DMA
    out = jax.ShapeDtypeStruct((length, width), bf16)
    dq, dk, dv, w = pl.pallas_call(
        functools.partial(kernel, n, m, scale, rscale),
        out_shape=(out, out, out, jax.ShapeDtypeStruct((rows, cb), f32)),
        in_specs=[vmem] * 5,
        out_specs=(vmem,) * 4,
        scratch_shapes=[
            pltpu.VMEM((n, length, wide), f32),
            pltpu.VMEM((n, length, wide), bf16),
            pltpu.VMEM((2, 2, half, HD, HD), f32),
            pltpu.VMEM((2, 2, half, HD, HD), f32),
            pltpu.VMEM((2, half, HD, HD), f32),
            pltpu.VMEM((max(chips - 1, 1), half, HD, HD), f32),
            pltpu.VMEM((2, 2, half, HD, HD), f32),
            pltpu.VMEM((3, length, width), f32),
            pltpu.VMEM((n, length, cb), f32),
            pltpu.VMEM((n, length, cb), f32),
            pltpu.VMEM((m, rows, cb), f32),
            pltpu.VMEM((max(m - 1, 1), rows, cb), f32),
            dma((2, n)), dma((2, n)),
            dma((2,)), dma((2,)),
            dma((max(chips - 1, 1),)), dma((max(chips - 1, 1),)),
            dma, dma,
            dma((n - 1,)), dma((n - 1,)),
            dma((max(m - 1, 1),)), dma((max(m - 1, 1),)),
        ],
        compiler_params=pltpu.CompilerParams(
            collective_id=0, has_side_effects=True, vmem_limit_bytes=56 * 2**20
        ),
    )(query_heads[0], key_heads[0], value_heads[0], grad_output[0], layer_input[0])
    return dq[None], dk[None], dv[None], w


def solution(mesh):
    spec = P("dp", "ctx", None)
    return jax.shard_map(
        on_device, mesh=mesh, in_specs=(spec,) * 5,
        out_specs=(spec, spec, spec, P("dp", "ctx")), check_vma=False,
    )
```

time: 178 us -> 63.9 us (0.36)
  waiting for transfers between devices: 138 us -> 0 us
  Pallas kernels: 0 us -> 57.6 us
  between operations: 13.9 us -> 0.65 us
  matrix products: 8.23 us -> 0 us
  other arithmetic: 8.21 us -> 0 us
  local copies, waits for them, and re-layouts: 8.78 us -> 4.42 us
    reduce_scatter x2 -> x0, waiting for transfers between devices: 75.8 us -> none  [the longest x1 57.1 us: on_device(): column_part = lax.psum_scatter(term, 'ctx', scatter_dimension=0, tiled=True)]
    all_gather x2 -> x0, waiting for transfers between devices: 62.1 us -> none  [entering(): gathered = lax.all_gather(part, axis)]
    pallas_call x0 -> x1, Pallas kernels: none -> 57.6 us  [on_device(): pl.pallas_call(functools.partial(kernel, n, m, scale, rscale), out_shape=...]
    dot_general x13 -> x0, matrix products: 8.23 us -> none  [the longest x1 2.89 us: on_device(): jnp.einsum('tr,tcw->crw', inputs, value_tiles, preferred_element_type=jnp...]
    add x7 -> x0, other arithmetic: 8.2 us -> none  [add_states(): return earlier + later]
    reduce_scatter x1 -> x0, local copies, waits for them, and re-layouts: 2.02 us -> none  [on_device(): column_part = lax.psum_scatter(term, 'ctx', scatter_dimension=0, tiled=True)]
    unnamed x8 -> x10, local copies, waits for them, and re-layouts: 5.54 us -> 4.42 us
  transfers between devices with their start and end apart: 4 -> 0, of which waited for: 4 -> 0; matrix products, arithmetic and copies ran while one was open for 11% -> 0% of each run, Pallas kernels for 0% -> 0%
where the time goes in v1:
time: 63.9 us; the launch traced here: 62.7 us
  Pallas kernels  57.6 us (90%)
  local copies, waits for them, and re-layouts  4.42 us (7%)
  between operations  0.65 us (1%)
    pallas_call x1, Pallas kernels, on_device(): pl.pallas_call(functools.partial(kernel, n, m, scale, rscale), out_shape=...  57.6 us
    unnamed x10, local copies, waits for them, and re-layouts  4.42 us

profile of v1, /device:TPU:0, one launch (start us, length us, event | category | flops | bytes accessed | tf_op | source)
XLA Modules:
  0.0 62.7 jit_solution(3451959931611888527)
XLA Ops:
  0.6 57.6 %shard_map.84 = (bf16[128,1024]{1,0:T(8,128)(2,1)}, bf16[128,1024]{1,0:T(8,128)(2,1)}, bf16[128,1024]{1,0:T(8,128)(2,1)}, f32[288,128]{1,0:T(8,128)}) custom-call(bf16[128,1024]{1,0:T(8,128)(2,1)} %bitcast.12, bf16[128,1024]{1,0:T(8,128)(2,1)} %bitcast.13, bf16[128,1024]{1,0:T(8,128)(2,1)} %bitcast.14, bf16[128,1024]{1,0:T(8,128)(2,1)} %bitcast.15, ...), custom_call_target="tpu_custom_call" | custom-call | tf_op jit(solution)/shard_map/pallas_call | solution.py:239
  58.3 0.0 copy-start.1
  58.3 1.7 %copy.13 = bf16[1,128,1024]{2,1,0:T(8,128)(2,1)} copy(bf16[1,128,1024]{2,1,0:T(8,128)(2,1)} %bitcast.11) | data formatting | bytes 524288
  60.0 0.0 copy-done.1
  60.0 0.0 copy-start
  60.0 0.7 %copy.14 = bf16[1,128,1024]{2,1,0:T(8,128)(2,1)} copy(bf16[1,128,1024]{2,1,0:T(8,128)(2,1)S(1)} %bitcast.10) | data formatting | bytes 524288
  60.7 0.3 copy-done
  61.0 0.0 copy-start.2
  61.0 0.7 %copy.15 = bf16[1,128,1024]{2,1,0:T(8,128)(2,1)} copy(bf16[1,128,1024]{2,1,0:T(8,128)(2,1)S(1)} %bitcast.9) | data formatting | bytes 524288
  61.7 0.3 copy-done.2
  62.0 0.7 %copy.16 = f32[288,128]{1,0:T(8,128)} copy(f32[288,128]{1,0:T(8,128)S(1)} %copy-done.2) | data formatting | bytes 294912
Async XLA Ops:
  58.3 1.7 %copy-start.1 = (bf16[128,1024]{1,0:T(8,128)(2,1)S(1)}, bf16[128,1024]{1,0:T(8,128)(2,1)}, u32[]{:S(2)}) copy-start(bf16[128,1024]{1,0:T(8,128)(2,1)} %get-tuple-element.9) | copy-start | bytes 786436
  60.0 1.0 %copy-start = (bf16[128,1024]{1,0:T(8,128)(2,1)S(1)}, bf16[128,1024]{1,0:T(8,128)(2,1)}, u32[]{:S(2)}) copy-start(bf16[128,1024]{1,0:T(8,128)(2,1)} %get-tuple-element.10) | copy-start | bytes 786436
  61.0 1.0 %copy-start.2 = (f32[288,128]{1,0:T(8,128)S(1)}, f32[288,128]{1,0:T(8,128)}, u32[]{:S(2)}) copy-start(f32[288,128]{1,0:T(8,128)} %get-tuple-element.19) | copy-start | bytes 442372

commit v2 on v1

v2 whole, which is shorter than its diff:
```python
import functools
import math

import jax
import jax.numpy as jnp
from jax import lax
from jax.experimental import pallas as pl
from jax.experimental.pallas import tpu as pltpu
from jax.sharding import PartitionSpec as P

HD = 128
NN = (((1,), (0,)), ((), ()))
NT = (((1,), (1,)), ((), ()))
TN = (((0,), (0,)), ((), ()))


def dot(a, b, dims):
    return lax.dot_general(a, b, dims, preferred_element_type=jnp.float32)


def kernel(
    n, m, scale, rscale,
    q, k, v, g, x,
    dq, dk, dv, w,
    xs, xsib, xt, st, sib, tot, srecv, ext, acc, dvs, dvr, wt, wr, wrecv,
    x_send, x_recv, p_send, p_recv, s_send, s_recv, e_send, e_recv,
    d_send, d_recv, r_send, r_recv, w_send, w_recv,
):
    length, width = q.shape
    heads = width // HD
    half = heads // 2
    chips = n // 2
    cb = dvs.shape[3]
    rows = w.shape[0]
    part = rows // 2
    bits = chips.bit_length() - 1
    me = lax.axis_index("ctx")
    row = lax.axis_index("dp")
    core = lax.rem(me, 2)
    chip = me // 2
    sibling = me + 1 - 2 * core

    def flip(mask):
        out = chip
        for b in range(bits):
            if mask >> b & 1:
                out = out + (1 << b) * (1 - 2 * lax.rem(chip // (1 << b), 2))
        return out

    def remote(src, dst, send, recv, to):
        return pltpu.make_async_remote_copy(
            src_ref=src, dst_ref=dst, send_sem=send, recv_sem=recv,
            device_id=to, device_id_type=pl.DeviceIdType.MESH,
        )

    orders = ([*range(bits)], [*range(bits - 1, -1, -1)])

    def place(s, mask):
        return sum((mask >> b & 1) << (bits - 1 - i) for i, b in enumerate(orders[s]))

    barrier = pltpu.get_barrier_semaphore()
    for j in range(1, n):
        pl.semaphore_signal(
            barrier, inc=1, device_id={"ctx": lax.rem(me + j, n)},
            device_id_type=pl.DeviceIdType.MESH,
        )
    for j in range(1, m):
        pl.semaphore_signal(
            barrier, inc=1, device_id={"dp": lax.rem(row + j, m)},
            device_id_type=pl.DeviceIdType.MESH,
        )

    def cols(h):
        return slice(h * HD, (h + 1) * HD)

    for h in range(heads):
        a, i = h // half, h % half
        st[a, 0, i] = dot(k[:, cols(h)], v[:, cols(h)], TN)
        st[a, 1, i] = dot(q[:, cols(h)], g[:, cols(h)], TN)
    xs[...] = x[...].astype(jnp.float32)
    pl.semaphore_wait(barrier, n - 1 + m - 1)

    pair = [
        remote(st.at[1 - core], sib.at[1 - core], p_send.at[0], p_recv.at[0], {"ctx": sibling}),
        remote(st.at[core], sib.at[core], p_send.at[1], p_recv.at[1], {"ctx": sibling}),
    ]
    pair_in = remote(st.at[core], sib.at[core], p_send.at[0], p_recv.at[0], {"ctx": sibling})
    for c in pair:
        c.start()
    x_pair = remote(xs, xsib, x_send, x_recv, {"ctx": sibling})
    pair_in.wait_recv()
    tot[...] = st[core] + sib[core]
    states = []
    for j in range(1, chips):
        wrap = (chip + j) // chips
        to = (chip + j - chips * wrap) * 2 + core
        c = remote(tot.at[wrap], srecv.at[j - 1], s_send.at[j - 1], s_recv.at[j - 1], {"ctx": to})
        c.start()
        states.append(c)
    x_pair.start()

    at_row = lax.broadcasted_iota(jnp.int32, (length, length), 0)
    at_col = lax.broadcasted_iota(jnp.int32, (length, length), 1)
    lower = at_row >= at_col
    upper = at_row <= at_col
    for h in range(heads):
        qh, kh, vh, gh = (r[:, cols(h)] for r in (q, k, v, g))
        score_t = jnp.where(upper, scale * dot(kh, qh, NT), 0.0).astype(jnp.bfloat16)
        grad = jnp.where(lower, scale * dot(gh, vh, NT), 0.0).astype(jnp.bfloat16)
        acc[0, :, cols(h)] = dot(grad, kh, NN)
        acc[1, :, cols(h)] = dot(grad, qh, TN)
        acc[2, :, cols(h)] = dot(score_t, gh, NN)

    xt[:, :length] = jnp.transpose(xs[...]).astype(jnp.bfloat16)
    x_pair.wait_recv()
    xt[:, length:] = jnp.transpose(xsib[...]).astype(jnp.bfloat16)

    ext[core] = jnp.zeros_like(tot)
    for j in range(1, chips):
        kind = 1 - (chip - j + chips) // chips
        states[j - 1].wait_recv()
        ext[core, kind] += srecv[j - 1]
    share = remote(ext.at[core], ext.at[core], e_send, e_recv, {"ctx": sibling})
    share_in = remote(ext.at[1 - core], ext.at[1 - core], e_send, e_recv, {"ctx": sibling})
    share.start()
    pair_rest = remote(st.at[1 - core], sib.at[1 - core], p_send.at[1], p_recv.at[1], {"ctx": sibling})
    pair_rest.wait_recv()
    share_in.wait_recv()

    second = core.astype(jnp.float32)
    first = 1.0 - second

    def suffix(h):
        a, i = h // half, h % half
        return (scale * (ext[a, 1, i] + first * sib[a, 1, i])).astype(jnp.bfloat16)

    def prefix(h):
        a, i = h // half, h % half
        return (scale * (ext[a, 0, i] + second * sib[a, 0, i])).astype(jnp.bfloat16)

    for h in range(heads):
        out = acc[2, :, cols(h)] + dot(k[:, cols(h)], suffix(h), NN)
        dv[:, cols(h)] = out.astype(jnp.bfloat16)
    for j in range(n):
        dvs[j % 2, j // 2] = dv[:, j * cb:(j + 1) * cb].astype(jnp.float32)
    value = remote(dvs.at[1 - core], dvr, d_send, d_recv, {"ctx": sibling})
    value.start()
    value.wait_recv()

    for mask in range(chips - 1, -1, -1):
        to = flip(mask)
        both = jnp.concatenate([dvs[core, to], dvr[to]], 0).astype(jnp.bfloat16)
        tile = dot(xt[...], both, NN)
        for d in range(m):
            for s in range(2):
                lo = d * rows + s * part
                wt[s, d, place(s, mask)] = tile[lo:lo + part]

    def chunk(c):
        return lax.rem(row + c + 1, m)

    def halve(s, c, i):
        lo = 1 << (bits - 1 - i)
        d = chunk(c)
        return remote(
            wt.at[s, d, pl.ds(lo, lo)], wr.at[s, d, pl.ds(lo, lo)],
            r_send.at[s, c, i], r_recv.at[s, c, i], {"ctx": flip(1 << orders[s][i]) * 2 + core},
        )

    def across(s, c):
        return remote(
            wt.at[s, chunk(c), 0], wrecv.at[s, c], w_send.at[s, c], w_recv.at[s, c],
            {"dp": chunk(c)},
        )

    def advance(s, c, i):
        d = chunk(c)
        if i > 0:
            lo = 1 << (bits - i)
            halve(s, c, i - 1).wait_recv()
            wt[s, d, 0:lo] += wr[s, d, lo:2 * lo]
        if i < bits:
            halve(s, c, i).start()
        elif c < m - 1:
            across(s, c).start()

    def step(t):
        for i in range(bits + 1):
            for s in range(2):
                if 0 <= t - i < m:
                    advance(s, t - i, i)

    for s in range(2):
        advance(s, 0, 0)

    for h in range(heads):
        out = acc[0, :, cols(h)] + dot(g[:, cols(h)], prefix(h), NT)
        dq[:, cols(h)] = out.astype(jnp.bfloat16)
        out = acc[1, :, cols(h)] + dot(v[:, cols(h)], suffix(h), NT)
        dk[:, cols(h)] = out.astype(jnp.bfloat16)

    for t in range(1, m + bits):
        step(t)
    for s in range(2):
        out = wt[s, row, 0]
        for c in range(m - 1):
            across(s, c).wait_recv()
            out = out + wrecv[s, c]
        w[s * part:(s + 1) * part] = out * rscale

    for c in pair + states + [x_pair, share, value]:
        c.wait_send()
    for s in range(2):
        for c in range(m):
            for i in range(bits):
                halve(s, c, i).wait_send()
            if c < m - 1:
                across(s, c).wait_send()


def copy_out(*refs):
    count = len(refs) // 2
    sems = refs[-1]
    copies = [pltpu.make_async_copy(refs[i], refs[count + i], sems.at[i]) for i in range(count)]
    for c in copies:
        c.start()
    for c in copies:
        c.wait()


def on_device(query_heads, key_heads, value_heads, grad_output, layer_input):
    length, width = query_heads.shape[1:]
    wide = layer_input.shape[2]
    n = lax.axis_size("ctx")
    m = lax.axis_size("dp")
    scale = 1.0 / math.sqrt(HD * length * n)
    rscale = 1.0 / math.sqrt(m * length * n)
    heads, chips, cb, rows = width // HD, n // 2, width // n, wide // m
    half, bits = heads // 2, chips.bit_length() - 1
    f32, bf16 = jnp.float32, jnp.bfloat16
    vmem = pl.BlockSpec(memory_space=pltpu.VMEM)
    dma = pltpu.SemaphoreType.DMA
    out = jax.ShapeDtypeStruct((length, width), bf16)
    dq, dk, dv, w = pl.pallas_call(
        functools.partial(kernel, n, m, scale, rscale),
        out_shape=(out, out, out, jax.ShapeDtypeStruct((rows, cb), f32)),
        in_specs=[vmem] * 5,
        out_specs=(vmem,) * 4,
        scratch_shapes=[
            pltpu.VMEM((length, wide), f32),
            pltpu.VMEM((length, wide), f32),
            pltpu.VMEM((wide, 2 * length), bf16),
            pltpu.VMEM((2, 2, half, HD, HD), f32),
            pltpu.VMEM((2, 2, half, HD, HD), f32),
            pltpu.VMEM((2, half, HD, HD), f32),
            pltpu.VMEM((max(chips - 1, 1), half, HD, HD), f32),
            pltpu.VMEM((2, 2, half, HD, HD), f32),
            pltpu.VMEM((3, length, width), f32),
            pltpu.VMEM((2, chips, length, cb), f32),
            pltpu.VMEM((chips, length, cb), f32),
            pltpu.VMEM((2, m, chips, rows // 2, cb), f32),
            pltpu.VMEM((2, m, chips, rows // 2, cb), f32),
            pltpu.VMEM((2, max(m - 1, 1), rows // 2, cb), f32),
            dma, dma,
            dma((2,)), dma((2,)),
            dma((max(chips - 1, 1),)), dma((max(chips - 1, 1),)),
            dma, dma,
            dma, dma,
            dma((2, m, max(bits, 1))), dma((2, m, max(bits, 1))),
            dma((2, max(m - 1, 1))), dma((2, max(m - 1, 1))),
        ],
        compiler_params=pltpu.CompilerParams(
            collective_id=0, has_side_effects=True, vmem_limit_bytes=56 * 2**20
        ),
    )(query_heads[0], key_heads[0], value_heads[0], grad_output[0], layer_input[0])
    made = (dq, dk, dv, w)
    dq, dk, dv, w = pl.pallas_call(
        copy_out,
        out_shape=tuple(jax.ShapeDtypeStruct(r.shape, r.dtype) for r in made),
        in_specs=[pl.BlockSpec(memory_space=pltpu.HBM)] * len(made),
        out_specs=(pl.BlockSpec(memory_space=pltpu.HBM),) * len(made),
        scratch_shapes=[dma((len(made),))],
    )(*made)
    return dq[None], dk[None], dv[None], w


def solution(mesh):
    spec = P("dp", "ctx", None)
    return jax.shard_map(
        on_device, mesh=mesh, in_specs=(spec,) * 5,
        out_specs=(spec, spec, spec, P("dp", "ctx")), check_vma=False,
    )
```

time: 63.9 us -> 82.9 us (1.30); the launches traced: 62.7 us -> 82.7 us
  Pallas kernels: 57.6 us -> 82.1 us
  local copies, waits for them, and re-layouts: 4.42 us -> 0 us
    pallas_call x0 -> x1, Pallas kernels: none -> 29.4 us  [on_device(): pl.pallas_call(copy_out, out_shape=tuple((jax.ShapeDtypeStruct(r.shape, r...]
    pallas_call x1, Pallas kernels: 57.6 us -> 52.7 us  [on_device(): pl.pallas_call(functools.partial(kernel, n, m, scale, rscale), out_shape=...]
    unnamed x10 -> x0, local copies, waits for them, and re-layouts: 4.42 us -> none
where the time goes in v2:
time: 82.9 us; the launch traced here: 82.7 us
  Pallas kernels  82.1 us (99%)
    pallas_call x1, Pallas kernels, on_device(): pl.pallas_call(functools.partial(kernel, n, m, scale, rscale), out_shape=...  52.7 us
    pallas_call x1, Pallas kernels, on_device(): pl.pallas_call(copy_out, out_shape=tuple((jax.ShapeDtypeStruct(r.shape, r...  29.4 us

profile of v2, /device:TPU:0, one launch (start us, length us, event | category | flops | bytes accessed | tf_op | source)
XLA Modules:
  0.0 82.7 jit_solution(14121758821872713362)
XLA Ops:
  0.6 52.7 %shard_map.84 = (bf16[128,1024]{1,0:T(8,128)(2,1)}, bf16[128,1024]{1,0:T(8,128)(2,1)}, bf16[128,1024]{1,0:T(8,128)(2,1)}, f32[288,128]{1,0:T(8,128)}) custom-call(bf16[128,1024]{1,0:T(8,128)(2,1)} %bitcast.9, bf16[128,1024]{1,0:T(8,128)(2,1)} %bitcast.10, bf16[128,1024]{1,0:T(8,128)(2,1)} %bitcast.11, bf16[128,1024]{1,0:T(8,128)(2,1)} %bitcast.12, ...), custom_call_target="tpu_custom_call" | custom-call | tf_op jit(solution)/shard_map/pallas_call | solution.py:244
  53.3 29.4 %shard_map.85 = (bf16[128,1024]{1,0:T(8,128)(2,1)}, bf16[128,1024]{1,0:T(8,128)(2,1)}, bf16[128,1024]{1,0:T(8,128)(2,1)}, f32[288,128]{1,0:T(8,128)}) custom-call(bf16[128,1024]{1,0:T(8,128)(2,1)} %get-tuple-element.12.refs_0_, bf16[128,1024]{1,0:T(8,128)(2,1)} %get-tuple-element.13.refs_1_, bf16[128,1024]{1,0:T(8,128)(2,1)} %get-tuple-element.14.refs_2_, ...), custom_call_target="tpu_custom_call" | custom-call | tf_op jit(solution)/shard_map/pallas_call | solution.py:277

commit v3 on v2

--- a/solution.py
+++ b/solution.py
@@ -219,12 +219,22 @@
 
 
 def copy_out(*refs):
-    count = len(refs) // 2
+    count = (len(refs) - 1) // 3
     sems = refs[-1]
-    copies = [pltpu.make_async_copy(refs[i], refs[count + i], sems.at[i]) for i in range(count)]
-    for c in copies:
+
+    def copies(source, target, at):
+        return [
+            pltpu.make_async_copy(refs[source * count + i], refs[target * count + i], sems.at[at, i])
+            for i in range(count)
+        ]
+
+    into, out = copies(0, 2, 0), copies(2, 1, 1)
+    for c in into:
         c.start()
-    for c in copies:
+    for i in range(count):
+        into[i].wait()
+        out[i].start()
+    for c in out:
         c.wait()
 
 
@@ -279,7 +289,7 @@
         out_shape=tuple(jax.ShapeDtypeStruct(r.shape, r.dtype) for r in made),
         in_specs=[pl.BlockSpec(memory_space=pltpu.HBM)] * len(made),
         out_specs=(pl.BlockSpec(memory_space=pltpu.HBM),) * len(made),
-        scratch_shapes=[dma((len(made),))],
+        scratch_shapes=[pltpu.VMEM(r.shape, r.dtype) for r in made] + [dma((2, len(made)))],
     )(*made)
     return dq[None], dk[None], dv[None], w
 

time: 82.9 us -> 55.4 us (0.67)
  Pallas kernels: 82.1 us -> 54.6 us
    pallas_call x1, Pallas kernels: 29.4 us -> 1.94 us  [on_device(): pl.pallas_call(copy_out, out_shape=tuple((jax.ShapeDtypeStruct(r.shape, r...]
where the time goes in v3:
time: 55.4 us; the launch traced here: 55.3 us
  Pallas kernels  54.6 us (99%)
  between operations  0.64 us (1%)
    pallas_call x1, Pallas kernels, on_device(): pl.pallas_call(functools.partial(kernel, n, m, scale, rscale), out_shape=...  52.7 us
    pallas_call x1, Pallas kernels, on_device(): pl.pallas_call(copy_out, out_shape=tuple((jax.ShapeDtypeStruct(r.shape, r...  1.94 us

profile of v3, /device:TPU:0, one launch (start us, length us, event | category | flops | bytes accessed | tf_op | source)
XLA Modules:
  0.0 55.3 jit_solution(12803601033792462538)
XLA Ops:
  0.6 52.7 %shard_map.84 = (bf16[128,1024]{1,0:T(8,128)(2,1)}, bf16[128,1024]{1,0:T(8,128)(2,1)}, bf16[128,1024]{1,0:T(8,128)(2,1)}, f32[288,128]{1,0:T(8,128)}) custom-call(bf16[128,1024]{1,0:T(8,128)(2,1)} %bitcast.9, bf16[128,1024]{1,0:T(8,128)(2,1)} %bitcast.10, bf16[128,1024]{1,0:T(8,128)(2,1)} %bitcast.11, bf16[128,1024]{1,0:T(8,128)(2,1)} %bitcast.12, ...), custom_call_target="tpu_custom_call" | custom-call | tf_op jit(solution)/shard_map/pallas_call | solution.py:254
  53.3 1.9 %shard_map.85 = (bf16[128,1024]{1,0:T(8,128)(2,1)}, bf16[128,1024]{1,0:T(8,128)(2,1)}, bf16[128,1024]{1,0:T(8,128)(2,1)}, f32[288,128]{1,0:T(8,128)}) custom-call(bf16[128,1024]{1,0:T(8,128)(2,1)} %get-tuple-element.12.refs_0_, bf16[128,1024]{1,0:T(8,128)(2,1)} %get-tuple-element.13.refs_1_, bf16[128,1024]{1,0:T(8,128)(2,1)} %get-tuple-element.14.refs_2_, ...), custom_call_target="tpu_custom_call" | custom-call | tf_op jit(solution)/shard_map/pallas_call | solution.py:287

commit v4 on v3

--- a/solution.py
+++ b/solution.py
@@ -22,7 +22,7 @@
     n, m, scale, rscale,
     q, k, v, g, x,
     dq, dk, dv, w,
-    xs, xsib, xt, st, sib, tot, srecv, ext, acc, dvs, dvr, wt, wr, wrecv,
+    xs, xsib, xt, st, sib, tot, srecv, ext, acc, gw, dvs, dvr, wt, wr, wrecv,
     x_send, x_recv, p_send, p_recv, s_send, s_recv, e_send, e_recv,
     d_send, d_recv, r_send, r_recv, w_send, w_recv,
 ):
@@ -73,59 +73,105 @@
     def cols(h):
         return slice(h * HD, (h + 1) * HD)
 
-    for h in range(heads):
-        a, i = h // half, h % half
-        st[a, 0, i] = dot(k[:, cols(h)], v[:, cols(h)], TN)
-        st[a, 1, i] = dot(q[:, cols(h)], g[:, cols(h)], TN)
+    def blocks(kind, left, right):
+        for h in range(heads):
+            st[h // half, kind, h % half] = dot(left[:, cols(h)], right[:, cols(h)], TN)
+
+    blocks(1, q, g)
     xs[...] = x[...].astype(jnp.float32)
     pl.semaphore_wait(barrier, n - 1 + m - 1)
 
-    pair = [
-        remote(st.at[1 - core], sib.at[1 - core], p_send.at[0], p_recv.at[0], {"ctx": sibling}),
-        remote(st.at[core], sib.at[core], p_send.at[1], p_recv.at[1], {"ctx": sibling}),
-    ]
-    pair_in = remote(st.at[core], sib.at[core], p_send.at[0], p_recv.at[0], {"ctx": sibling})
-    for c in pair:
+    def pair(a, kind, at):
+        return remote(st.at[a, kind], sib.at[a, kind], p_send.at[at], p_recv.at[at], {"ctx": sibling})
+
+    pairs = [pair(1 - core, 1, 0), pair(1 - core, 0, 1), pair(core, 1, 2), pair(core, 0, 3)]
+    pairs_in = [pair(core, 1, 0), pair(core, 0, 1), pair(1 - core, 1, 2), pair(1 - core, 0, 3)]
+    x_pair = remote(xs, xsib, x_send, x_recv, {"ctx": sibling})
+    pairs[0].start()
+    blocks(0, k, v)
+
+    def bit(i):
+        return lax.rem(chip // (1 << i), 2)
+
+    def sends(kind, i):
+        above = chip // (1 << (i + 1))
+        if kind:
+            return (bit(i) == 1) | (above != 0)
+        return (bit(i) == 0) | (above != (chips >> (i + 1)) - 1)
+
+    def takes(kind, i):
+        above = chip // (1 << (i + 1))
+        if kind:
+            return (bit(i) == 0) | (above != 0)
+        return (bit(i) == 1) | (above != (chips >> (i + 1)) - 1)
+
+    def scan_copy(kind, i, c):
+        return remote(
+            tot.at[kind, i, c], srecv.at[kind, i, c],
+            s_send.at[kind, i, c], s_recv.at[kind, i, c], {"ctx": flip(1 << i) * 2 + core},
+        )
+
+    def scan_send(kind, i, c):
+        @pl.when(sends(kind, i))
+        def _():
+            scan_copy(kind, i, c).start()
+
+    def scan_take(kind, i, c):
+        @pl.when(takes(kind, i))
+        def _():
+            scan_copy(kind, i, c).wait_recv()
+
+            @pl.when(bit(i) == 1 - kind)
+            def _():
+                ext[core, kind, c] += srecv[kind, i, c]
+
+            if i < bits - 1:
+                tot[kind, i + 1, c] = tot[kind, i, c] + srecv[kind, i, c]
+
+        if i < bits - 1:
+            scan_send(kind, i + 1, c)
+
+    def scan_begin(kind):
+        pairs_in[1 - kind].wait_recv()
+        for c in range(half):
+            tot[kind, 0, c] = st[core, kind, c] + sib[core, kind, c]
+            if bits > 0:
+                scan_send(kind, 0, c)
+
+    def share(a, kind):
+        return remote(ext.at[a, kind], ext.at[a, kind], e_send.at[kind], e_recv.at[kind], {"ctx": sibling})
+
+    ext[core] = jnp.zeros((2, half, HD, HD), jnp.float32)
+    scan_begin(1)
+    for c in pairs[1:]:
         c.start()
-    x_pair = remote(xs, xsib, x_send, x_recv, {"ctx": sibling})
-    pair_in.wait_recv()
-    tot[...] = st[core] + sib[core]
-    states = []
-    for j in range(1, chips):
-        wrap = (chip + j) // chips
-        to = (chip + j - chips * wrap) * 2 + core
-        c = remote(tot.at[wrap], srecv.at[j - 1], s_send.at[j - 1], s_recv.at[j - 1], {"ctx": to})
-        c.start()
-        states.append(c)
     x_pair.start()
 
     at_row = lax.broadcasted_iota(jnp.int32, (length, length), 0)
     at_col = lax.broadcasted_iota(jnp.int32, (length, length), 1)
     lower = at_row >= at_col
     upper = at_row <= at_col
-    for h in range(heads):
-        qh, kh, vh, gh = (r[:, cols(h)] for r in (q, k, v, g))
-        score_t = jnp.where(upper, scale * dot(kh, qh, NT), 0.0).astype(jnp.bfloat16)
-        grad = jnp.where(lower, scale * dot(gh, vh, NT), 0.0).astype(jnp.bfloat16)
-        acc[0, :, cols(h)] = dot(grad, kh, NN)
-        acc[1, :, cols(h)] = dot(grad, qh, TN)
-        acc[2, :, cols(h)] = dot(score_t, gh, NN)
-
+
+    def value_inside(heads_now):
+        for h in heads_now:
+            score_t = jnp.where(upper, scale * dot(k[:, cols(h)], q[:, cols(h)], NT), 0.0)
+            acc[:, cols(h)] = dot(score_t.astype(jnp.bfloat16), g[:, cols(h)], NN)
+
+    value_inside(range(half))
     xt[:, :length] = jnp.transpose(xs[...]).astype(jnp.bfloat16)
+    if bits > 0:
+        for c in range(half):
+            scan_take(1, 0, c)
+    scan_begin(0)
+    value_inside(range(half, heads))
     x_pair.wait_recv()
     xt[:, length:] = jnp.transpose(xsib[...]).astype(jnp.bfloat16)
-
-    ext[core] = jnp.zeros_like(tot)
-    for j in range(1, chips):
-        kind = 1 - (chip - j + chips) // chips
-        states[j - 1].wait_recv()
-        ext[core, kind] += srecv[j - 1]
-    share = remote(ext.at[core], ext.at[core], e_send, e_recv, {"ctx": sibling})
-    share_in = remote(ext.at[1 - core], ext.at[1 - core], e_send, e_recv, {"ctx": sibling})
-    share.start()
-    pair_rest = remote(st.at[1 - core], sib.at[1 - core], p_send.at[1], p_recv.at[1], {"ctx": sibling})
-    pair_rest.wait_recv()
-    share_in.wait_recv()
+    for i in range(1, bits):
+        for c in range(half):
+            scan_take(1, i, c)
+    share(core, 1).start()
+    pairs_in[2].wait_recv()
+    share(1 - core, 1).wait_recv()
 
     second = core.astype(jnp.float32)
     first = 1.0 - second
@@ -139,22 +185,16 @@
         return (scale * (ext[a, 0, i] + second * sib[a, 0, i])).astype(jnp.bfloat16)
 
     for h in range(heads):
-        out = acc[2, :, cols(h)] + dot(k[:, cols(h)], suffix(h), NN)
+        out = acc[:, cols(h)] + dot(k[:, cols(h)], suffix(h), NN)
         dv[:, cols(h)] = out.astype(jnp.bfloat16)
     for j in range(n):
         dvs[j % 2, j // 2] = dv[:, j * cb:(j + 1) * cb].astype(jnp.float32)
     value = remote(dvs.at[1 - core], dvr, d_send, d_recv, {"ctx": sibling})
     value.start()
+    if bits > 0:
+        for c in range(half):
+            scan_take(0, 0, c)
     value.wait_recv()
-
-    for mask in range(chips - 1, -1, -1):
-        to = flip(mask)
-        both = jnp.concatenate([dvs[core, to], dvr[to]], 0).astype(jnp.bfloat16)
-        tile = dot(xt[...], both, NN)
-        for d in range(m):
-            for s in range(2):
-                lo = d * rows + s * part
-                wt[s, d, place(s, mask)] = tile[lo:lo + part]
 
     def chunk(c):
         return lax.rem(row + c + 1, m)
@@ -184,23 +224,59 @@
         elif c < m - 1:
             across(s, c).start()
 
-    def step(t):
+    for mask in range(chips - 1, -1, -1):
+        to = flip(mask)
+        both = jnp.concatenate([dvs[core, to], dvr[to]], 0).astype(jnp.bfloat16)
+        tile = dot(xt[...], both, NN)
+        for d in range(m):
+            for s in range(2):
+                lo = d * rows + s * part
+                wt[s, d, place(s, mask)] = tile[lo:lo + part]
+        for s in range(2):
+            if bits > 0 and mask == 1 << orders[s][0]:
+                advance(s, 0, 0)
+
+    def key_out(heads_now):
+        for h in heads_now:
+            grad = jnp.where(lower, scale * dot(g[:, cols(h)], v[:, cols(h)], NT), 0.0)
+            gw[h] = grad.astype(jnp.bfloat16)
+            out = dot(gw[h], q[:, cols(h)], TN) + dot(v[:, cols(h)], suffix(h), NT)
+            dk[:, cols(h)] = out.astype(jnp.bfloat16)
+
+    def prefix_in():
+        for i in range(1, bits):
+            for c in range(half):
+                scan_take(0, i, c)
+        share(core, 0).start()
+
+    def query_out(heads_now):
+        for h in heads_now:
+            out = dot(gw[h], k[:, cols(h)], NN) + dot(g[:, cols(h)], prefix(h), NT)
+            dq[:, cols(h)] = out.astype(jnp.bfloat16)
+
+    def prefix_done():
+        pairs_in[3].wait_recv()
+        share(1 - core, 0).wait_recv()
+        query_out(range(half))
+
+    pieces = [
+        lambda: key_out(range(half)),
+        lambda: (prefix_in(), key_out(range(half, heads))),
+        prefix_done,
+        lambda: query_out(range(half, heads)),
+    ]
+    if bits == 0:
+        for s in range(2):
+            advance(s, 0, 0)
+    for t in range(1, m + bits):
         for i in range(bits + 1):
             for s in range(2):
                 if 0 <= t - i < m:
                     advance(s, t - i, i)
-
-    for s in range(2):
-        advance(s, 0, 0)
-
-    for h in range(heads):
-        out = acc[0, :, cols(h)] + dot(g[:, cols(h)], prefix(h), NT)
-        dq[:, cols(h)] = out.astype(jnp.bfloat16)
-        out = acc[1, :, cols(h)] + dot(v[:, cols(h)], suffix(h), NT)
-        dk[:, cols(h)] = out.astype(jnp.bfloat16)
-
-    for t in range(1, m + bits):
-        step(t)
+            if i == 0 and pieces:
+                pieces.pop(0)()
+    for piece in pieces:
+        piece()
     for s in range(2):
         out = wt[s, row, 0]
         for c in range(m - 1):
@@ -208,8 +284,14 @@
             out = out + wrecv[s, c]
         w[s * part:(s + 1) * part] = out * rscale
 
-    for c in pair + states + [x_pair, share, value]:
+    for c in pairs + [x_pair, share(core, 0), share(core, 1), value]:
         c.wait_send()
+    for kind in range(2):
+        for i in range(bits):
+            @pl.when(sends(kind, i))
+            def _():
+                for c in range(half):
+                    scan_copy(kind, i, c).wait_send()
     for s in range(2):
         for c in range(m):
             for i in range(bits):
@@ -262,19 +344,20 @@
             pltpu.VMEM((wide, 2 * length), bf16),
             pltpu.VMEM((2, 2, half, HD, HD), f32),
             pltpu.VMEM((2, 2, half, HD, HD), f32),
-            pltpu.VMEM((2, half, HD, HD), f32),
-            pltpu.VMEM((max(chips - 1, 1), half, HD, HD), f32),
+            pltpu.VMEM((2, max(bits, 1), half, HD, HD), f32),
+            pltpu.VMEM((2, max(bits, 1), half, HD, HD), f32),
             pltpu.VMEM((2, 2, half, HD, HD), f32),
-            pltpu.VMEM((3, length, width), f32),
+            pltpu.VMEM((length, width), f32),
+            pltpu.VMEM((heads, length, length), bf16),
             pltpu.VMEM((2, chips, length, cb), f32),
             pltpu.VMEM((chips, length, cb), f32),
             pltpu.VMEM((2, m, chips, rows // 2, cb), f32),
             pltpu.VMEM((2, m, chips, rows // 2, cb), f32),
             pltpu.VMEM((2, max(m - 1, 1), rows // 2, cb), f32),
             dma, dma,
+            dma((4,)), dma((4,)),
+            dma((2, max(bits, 1), half)), dma((2, max(bits, 1), half)),
             dma((2,)), dma((2,)),
-            dma((max(chips - 1, 1),)), dma((max(chips - 1, 1),)),
-            dma, dma,
             dma, dma,
             dma((2, m, max(bits, 1))), dma((2, m, max(bits, 1))),
             dma((2, max(m - 1, 1))), dma((2, max(m - 1, 1))),

time: 55.4 us -> 55.3 us (level)
  the two profiles are of different devices: /device:TPU:0 before, /device:TPU:5 now
where the time goes in v4:
time: 55.3 us; the launch traced here: 55.2 us
  Pallas kernels  54.5 us (99%)
  between operations  0.64 us (1%)
    pallas_call x1, Pallas kernels, on_device(): pl.pallas_call(functools.partial(kernel, n, m, scale, rscale), out_shape=...  52.6 us
    pallas_call x1, Pallas kernels, on_device(): pl.pallas_call(copy_out, out_shape=tuple((jax.ShapeDtypeStruct(r.shape, r...  1.94 us

profile of v4, /device:TPU:5, one launch (start us, length us, event | category | flops | bytes accessed | tf_op | source)
XLA Modules:
  0.0 55.2 jit_solution(12604000048421104783)
XLA Ops:
  0.6 52.6 %shard_map.84 = (bf16[128,1024]{1,0:T(8,128)(2,1)}, bf16[128,1024]{1,0:T(8,128)(2,1)}, bf16[128,1024]{1,0:T(8,128)(2,1)}, f32[288,128]{1,0:T(8,128)}) custom-call(bf16[128,1024]{1,0:T(8,128)(2,1)} %bitcast.9, bf16[128,1024]{1,0:T(8,128)(2,1)} %bitcast.10, bf16[128,1024]{1,0:T(8,128)(2,1)} %bitcast.11, bf16[128,1024]{1,0:T(8,128)(2,1)} %bitcast.12, ...), custom_call_target="tpu_custom_call" | custom-call | tf_op jit(solution)/shard_map/pallas_call | solution.py:336
  53.2 1.9 %shard_map.85 = (bf16[128,1024]{1,0:T(8,128)(2,1)}, bf16[128,1024]{1,0:T(8,128)(2,1)}, bf16[128,1024]{1,0:T(8,128)(2,1)}, f32[288,128]{1,0:T(8,128)}) custom-call(bf16[128,1024]{1,0:T(8,128)(2,1)} %get-tuple-element.12.refs_0_, bf16[128,1024]{1,0:T(8,128)(2,1)} %get-tuple-element.13.refs_1_, bf16[128,1024]{1,0:T(8,128)(2,1)} %get-tuple-element.14.refs_2_, ...), custom_call_target="tpu_custom_call" | custom-call | tf_op jit(solution)/shard_map/pallas_call | solution.py:370

commit v5 on v4

--- a/solution.py
+++ b/solution.py
@@ -191,9 +191,6 @@
         dvs[j % 2, j // 2] = dv[:, j * cb:(j + 1) * cb].astype(jnp.float32)
     value = remote(dvs.at[1 - core], dvr, d_send, d_recv, {"ctx": sibling})
     value.start()
-    if bits > 0:
-        for c in range(half):
-            scan_take(0, 0, c)
     value.wait_recv()
 
     def chunk(c):
@@ -224,17 +221,32 @@
         elif c < m - 1:
             across(s, c).start()
 
-    for mask in range(chips - 1, -1, -1):
-        to = flip(mask)
-        both = jnp.concatenate([dvs[core, to], dvr[to]], 0).astype(jnp.bfloat16)
-        tile = dot(xt[...], both, NN)
-        for d in range(m):
-            for s in range(2):
-                lo = d * rows + s * part
-                wt[s, d, place(s, mask)] = tile[lo:lo + part]
+    def tiles(masks):
+        both = jnp.concatenate([
+            jnp.concatenate([dvs[core, flip(mask)], dvr[flip(mask)]], 0).astype(jnp.bfloat16)
+            for mask in masks
+        ], 1)
+        made = dot(xt[...], both, NN)
+        for at, mask in enumerate(masks):
+            for d in range(m):
+                for s in range(2):
+                    lo = d * rows + s * part
+                    wt[s, d, place(s, mask)] = made[lo:lo + part, at * cb:(at + 1) * cb]
+
+    masks = [*range(chips - 1, 0, -2), *range(chips - 2, -1, -2)]
+    wide = 2 if chips > 1 else 1
+    ready, begun = set(), set()
+    for at in range(0, chips, wide):
+        tiles(masks[at:at + wide])
+        ready.update(masks[at:at + wide])
         for s in range(2):
-            if bits > 0 and mask == 1 << orders[s][0]:
+            need = {r for r in range(chips) if bits == 0 or r >> orders[s][0] & 1}
+            if need <= ready and s not in begun:
+                begun.add(s)
                 advance(s, 0, 0)
+    for s in range(2):
+        if bits > 0 and m > 1:
+            advance(s, 1, 0)
 
     def key_out(heads_now):
         for h in heads_now:
@@ -243,6 +255,11 @@
             out = dot(gw[h], q[:, cols(h)], TN) + dot(v[:, cols(h)], suffix(h), NT)
             dk[:, cols(h)] = out.astype(jnp.bfloat16)
 
+    def prefix_begin():
+        if bits > 0:
+            for c in range(half):
+                scan_take(0, 0, c)
+
     def prefix_in():
         for i in range(1, bits):
             for c in range(half):
@@ -261,18 +278,18 @@
 
     pieces = [
         lambda: key_out(range(half)),
-        lambda: (prefix_in(), key_out(range(half, heads))),
+        lambda: (prefix_begin(), key_out(range(half, heads))),
+        prefix_in,
         prefix_done,
         lambda: query_out(range(half, heads)),
     ]
-    if bits == 0:
-        for s in range(2):
-            advance(s, 0, 0)
+    lead = 1 if bits > 0 else 0
     for t in range(1, m + bits):
         for i in range(bits + 1):
+            c = t - i + (lead if i == 0 else 0)
             for s in range(2):
-                if 0 <= t - i < m:
-                    advance(s, t - i, i)
+                if 0 <= c < m:
+                    advance(s, c, i)
             if i == 0 and pieces:
                 pieces.pop(0)()
     for piece in pieces:

time: 55.3 us -> 58.6 us (1.060)
  the two profiles are of different devices: /device:TPU:5 before, /device:TPU:28 now
where the time goes in v5:
time: 58.6 us; the launch traced here: 58.4 us
  Pallas kernels  57.8 us (99%)
  between operations  0.64 us (1%)
    pallas_call x1, Pallas kernels, on_device(): pl.pallas_call(functools.partial(kernel, n, m, scale, rscale), out_shape=...  55.8 us
    pallas_call x1, Pallas kernels, on_device(): pl.pallas_call(copy_out, out_shape=tuple((jax.ShapeDtypeStruct(r.shape, r...  1.94 us

profile of v5, /device:TPU:28, one launch (start us, length us, event | category | flops | bytes accessed | tf_op | source)
XLA Modules:
  0.0 58.4 jit_solution(18414631431747218385)
XLA Ops:
  0.6 55.8 %shard_map.84 = (bf16[128,1024]{1,0:T(8,128)(2,1)}, bf16[128,1024]{1,0:T(8,128)(2,1)}, bf16[128,1024]{1,0:T(8,128)(2,1)}, f32[288,128]{1,0:T(8,128)}) custom-call(bf16[128,1024]{1,0:T(8,128)(2,1)} %bitcast.9, bf16[128,1024]{1,0:T(8,128)(2,1)} %bitcast.10, bf16[128,1024]{1,0:T(8,128)(2,1)} %bitcast.11, bf16[128,1024]{1,0:T(8,128)(2,1)} %bitcast.12, ...), custom_call_target="tpu_custom_call" | custom-call | tf_op jit(solution)/shard_map/pallas_call | solution.py:353
  56.5 1.9 %shard_map.85 = (bf16[128,1024]{1,0:T(8,128)(2,1)}, bf16[128,1024]{1,0:T(8,128)(2,1)}, bf16[128,1024]{1,0:T(8,128)(2,1)}, f32[288,128]{1,0:T(8,128)}) custom-call(bf16[128,1024]{1,0:T(8,128)(2,1)} %get-tuple-element.12.refs_0_, bf16[128,1024]{1,0:T(8,128)(2,1)} %get-tuple-element.13.refs_1_, bf16[128,1024]{1,0:T(8,128)(2,1)} %get-tuple-element.14.refs_2_, ...), custom_call_target="tpu_custom_call" | custom-call | tf_op jit(solution)/shard_map/pallas_call | solution.py:387

commit v6 on v3

--- a/solution.py
+++ b/solution.py
@@ -104,12 +104,9 @@
     lower = at_row >= at_col
     upper = at_row <= at_col
     for h in range(heads):
-        qh, kh, vh, gh = (r[:, cols(h)] for r in (q, k, v, g))
+        qh, kh, gh = (r[:, cols(h)] for r in (q, k, g))
         score_t = jnp.where(upper, scale * dot(kh, qh, NT), 0.0).astype(jnp.bfloat16)
-        grad = jnp.where(lower, scale * dot(gh, vh, NT), 0.0).astype(jnp.bfloat16)
-        acc[0, :, cols(h)] = dot(grad, kh, NN)
-        acc[1, :, cols(h)] = dot(grad, qh, TN)
-        acc[2, :, cols(h)] = dot(score_t, gh, NN)
+        acc[:, cols(h)] = dot(score_t, gh, NN)
 
     xt[:, :length] = jnp.transpose(xs[...]).astype(jnp.bfloat16)
     x_pair.wait_recv()
@@ -139,7 +136,7 @@
         return (scale * (ext[a, 0, i] + second * sib[a, 0, i])).astype(jnp.bfloat16)
 
     for h in range(heads):
-        out = acc[2, :, cols(h)] + dot(k[:, cols(h)], suffix(h), NN)
+        out = acc[:, cols(h)] + dot(k[:, cols(h)], suffix(h), NN)
         dv[:, cols(h)] = out.astype(jnp.bfloat16)
     for j in range(n):
         dvs[j % 2, j // 2] = dv[:, j * cb:(j + 1) * cb].astype(jnp.float32)
@@ -193,14 +190,24 @@
     for s in range(2):
         advance(s, 0, 0)
 
-    for h in range(heads):
-        out = acc[0, :, cols(h)] + dot(g[:, cols(h)], prefix(h), NT)
-        dq[:, cols(h)] = out.astype(jnp.bfloat16)
-        out = acc[1, :, cols(h)] + dot(v[:, cols(h)], suffix(h), NT)
-        dk[:, cols(h)] = out.astype(jnp.bfloat16)
-
+    def inputs_out(h):
+        qh, kh, vh, gh = (r[:, cols(h)] for r in (q, k, v, g))
+        grad = jnp.where(lower, scale * dot(gh, vh, NT), 0.0).astype(jnp.bfloat16)
+        dq[:, cols(h)] = (dot(grad, kh, NN) + dot(gh, prefix(h), NT)).astype(jnp.bfloat16)
+        dk[:, cols(h)] = (dot(grad, qh, TN) + dot(vh, suffix(h), NT)).astype(jnp.bfloat16)
+
+    todo = [*range(heads)]
     for t in range(1, m + bits):
-        step(t)
+        for i in range(bits + 1):
+            for s in range(2):
+                if 0 <= t - i < m:
+                    advance(s, t - i, i)
+            if i == 0:
+                for h in todo[:2]:
+                    inputs_out(h)
+                todo = todo[2:]
+    for h in todo:
+        inputs_out(h)
     for s in range(2):
         out = wt[s, row, 0]
         for c in range(m - 1):
@@ -265,7 +272,7 @@
             pltpu.VMEM((2, half, HD, HD), f32),
             pltpu.VMEM((max(chips - 1, 1), half, HD, HD), f32),
             pltpu.VMEM((2, 2, half, HD, HD), f32),
-            pltpu.VMEM((3, length, width), f32),
+            pltpu.VMEM((length, width), f32),
             pltpu.VMEM((2, chips, length, cb), f32),
             pltpu.VMEM((chips, length, cb), f32),
             pltpu.VMEM((2, m, chips, rows // 2, cb), f32),

time: 55.4 us -> 55.4 us (level)
  no operation moved by 1% of the time
where the time goes in v6:
time: 55.4 us; the launch traced here: 55.3 us
  Pallas kernels  54.6 us (99%)
  between operations  0.64 us (1%)
    pallas_call x1, Pallas kernels, on_device(): pl.pallas_call(functools.partial(kernel, n, m, scale, rscale), out_shape=...  52.7 us
    pallas_call x1, Pallas kernels, on_device(): pl.pallas_call(copy_out, out_shape=tuple((jax.ShapeDtypeStruct(r.shape, r...  1.94 us

profile of v6, /device:TPU:0, one launch (start us, length us, event | category | flops | bytes accessed | tf_op | source)
XLA Modules:
  0.0 55.3 jit_solution(12167084719168030882)
XLA Ops:
  0.6 52.7 %shard_map.84 = (bf16[128,1024]{1,0:T(8,128)(2,1)}, bf16[128,1024]{1,0:T(8,128)(2,1)}, bf16[128,1024]{1,0:T(8,128)(2,1)}, f32[288,128]{1,0:T(8,128)}) custom-call(bf16[128,1024]{1,0:T(8,128)(2,1)} %bitcast.9, bf16[128,1024]{1,0:T(8,128)(2,1)} %bitcast.10, bf16[128,1024]{1,0:T(8,128)(2,1)} %bitcast.11, bf16[128,1024]{1,0:T(8,128)(2,1)} %bitcast.12, ...), custom_call_target="tpu_custom_call" | custom-call | tf_op jit(solution)/shard_map/pallas_call | solution.py:261
  53.3 1.9 %shard_map.85 = (bf16[128,1024]{1,0:T(8,128)(2,1)}, bf16[128,1024]{1,0:T(8,128)(2,1)}, bf16[128,1024]{1,0:T(8,128)(2,1)}, f32[288,128]{1,0:T(8,128)}) custom-call(bf16[128,1024]{1,0:T(8,128)(2,1)} %get-tuple-element.12.refs_0_, bf16[128,1024]{1,0:T(8,128)(2,1)} %get-tuple-element.13.refs_1_, bf16[128,1024]{1,0:T(8,128)(2,1)} %get-tuple-element.14.refs_2_, ...), custom_call_target="tpu_custom_call" | custom-call | tf_op jit(solution)/shard_map/pallas_call | solution.py:294
